TPU v7x, 32 devices: a whole 2x2x4 slice. The times are simulated.
32 devices in a mesh: dom: 16 (over z, y, core), sub: 2 (over x).
Axes of the slice: x: 2, y: 2, z: 4, core: 2. Of those that a mesh axis runs over, the one named last changes fastest.
Arguments:
- dof_state: float32 [56, 9, 4096], P(None, None, ('dom', 'sub')), may hold values from -6 to 6
- stiffness: float32 [3, 56, 56], replicated, may hold values from -0.75 to 0.75
- face_proj: float32 [4, 21, 56], replicated, may hold values from -0.75 to 0.75
- face_lift: float32 [4, 56, 21], replicated, may hold values from -1 to 1
- face_rotate: float32 [3, 21, 21], replicated, may hold values from -1.25 to 1.25
- jacobians: float32 [16, 3, 9, 9], replicated, may hold values from -2 to 2
- material: int32 [4096], P(('dom', 'sub')), may hold values from 0 to 15
- inv_jacobian: float32 [3, 3, 4096], P(None, None, ('dom', 'sub')), may hold values from -2.5 to 2.5
- flux_own: float32 [4, 9, 9, 4096], P(None, None, None, ('dom', 'sub')), may hold values from -1.5 to 1.5
- flux_across: float32 [4, 9, 9, 4096], P(None, None, None, ('dom', 'sub')), may hold values from -1.5 to 1.5
- cluster: int32 [4096], P(('dom', 'sub')), may hold values from 0 to 1, as said below
- neighbour: int32 [4, 4096], P(None, ('dom', 'sub')), may hold values from 0 to 176, as said below
- across_face: int32 [4, 4096], P(None, ('dom', 'sub')), may hold values from 0 to 3
- rotation: int32 [4, 4096], P(None, ('dom', 'sub')), may hold values from 0 to 2
- send_list: int32 [1536], P(('dom', 'sub')), may hold values from 0 to 127
Outputs:
- dof_out: float32 [56, 9, 4096], P(None, None, ('dom', 'sub'))
Inputs may be any that keep to these rules, and one draw needn't show every extreme that they name: `cluster`: each partition of 128 elements has at most 64 fine elements, and some partition has exactly 64. `neighbour`: values below 128 are the partition's own elements, never the element itself; 128 + g is received slot g; 176 is an outflow face. Every received slot whose source partition exists is named by exactly one face of the partition.
All inputs are finite; a program needn't handle non-finite values.
Results may differ from a plain program's by a relative error of at most 0.0003.
Values sent between devices are 32-bit elements; how exact they have to be, the bound alone decides.
A program may use at most 64 MiB of HBM per device.

v0:
```python
import math

import jax
import jax.numpy as jnp
from jax import lax
from jax.sharding import PartitionSpec as P

ORDER = 6


HIGH = lax.Precision.HIGHEST


def padded(block, sides, width):
    for axis, dim in sides:
        count = lax.axis_size(axis)
        forward = [(i, i + 1) for i in range(count - 1)]
        backward = [(target, source) for source, target in forward]
        low = lax.ppermute(
            lax.slice_in_dim(block, block.shape[dim] - width, None, axis=dim), axis, forward
        )
        high = lax.ppermute(lax.slice_in_dim(block, 0, width, axis=dim), axis, backward)
        block = jnp.concatenate([low, block, high], axis=dim)
    return block


def mix_fields(data, mats):
    return jnp.sum(data[:, :, None, :] * mats[None], axis=1)


def star_of(inv_jacobian, jacobians, material):
    nmat = jacobians.shape[0]
    fields = jacobians.shape[2]
    picked = (material[None, :] == jnp.arange(nmat, dtype=jnp.int32)[:, None]).astype(jnp.float32)
    table = jnp.transpose(jacobians.reshape(nmat, 3 * fields * fields))
    per_elem = jnp.dot(table, picked, precision=HIGH).reshape(3, fields, fields, material.shape[0])
    stacked = []
    for dim_d in range(3):
        summed = inv_jacobian[0, dim_d][None, None, :] * per_elem[0]
        for dim_c in range(1, 3):
            summed = summed + inv_jacobian[dim_c, dim_d][None, None, :] * per_elem[dim_c]
        stacked.append(summed)
    return jnp.stack(stacked)


def derivative(state, stiffness, star_mats):
    total = None
    for dim_d in range(3):
        moved = jnp.einsum("xb,xqe->bqe", stiffness[dim_d], state, precision=HIGH)
        term = mix_fields(moved, star_mats[dim_d])
        total = term if total is None else total + term
    return -total


def taylor(state, stiffness, star_mats):
    series = [state]
    for order in range(ORDER - 1):
        series.append(derivative(series[-1], stiffness, star_mats))
    return series


def integral(series, start_time, end_time):
    summed = jnp.zeros_like(series[0])
    for order in range(len(series)):
        factor = (end_time ** (order + 1) - start_time ** (order + 1)) / math.factorial(order + 1)
        summed = summed + factor * series[order]
    return summed


def volume(own_integral, stiffness, star_mats):
    total = None
    for dim_d in range(3):
        weighted = mix_fields(own_integral, star_mats[dim_d])
        term = jnp.einsum("bx,xpe->bpe", stiffness[dim_d], weighted, precision=HIGH)
        total = term if total is None else total + term
    return total


def lift_faces(solved_list, face_lift):
    faces, basis, face_basis = face_lift.shape
    lifter = jnp.transpose(face_lift, (1, 0, 2)).reshape(basis, faces * face_basis)
    return jnp.einsum("bg,gpe->bpe", lifter, jnp.concatenate(solved_list, axis=0), precision=HIGH)


def local_faces(own_integral, face_proj, face_lift, flux_own):
    faces, face_basis, basis = face_proj.shape
    projected = jnp.einsum(
        "gx,xqe->gqe", face_proj.reshape(faces * face_basis, basis), own_integral, precision=HIGH
    )
    solved_list = [
        mix_fields(projected[i * face_basis : (i + 1) * face_basis], flux_own[i])
        for i in range(faces)
    ]
    return lift_faces(solved_list, face_lift)


def neighbour_faces(
    near_list, across_face, rotation, face_proj, face_lift, face_rotate, flux_across
):
    faces, face_basis, basis = face_proj.shape
    combos = jnp.einsum("hfg,jgx->hjfx", face_rotate, face_proj, precision=HIGH).reshape(
        12 * face_basis, basis
    )
    solved_list = []
    for i in range(faces):
        near = near_list[i]
        projected = jnp.einsum("gx,xqe->gqe", combos, near, precision=HIGH)
        projected = projected.reshape(12, face_basis, near.shape[1], near.shape[2])
        choice_key = rotation[i] * 4 + across_face[i]
        pick = (choice_key[None, :] == jnp.arange(12, dtype=jnp.int32)[:, None]).astype(jnp.float32)
        chosen = jnp.sum(projected * pick[:, None, None, :], axis=0)
        solved_list.append(mix_fields(chosen, flux_across[i]))
    return lift_faces(solved_list, face_lift)


def update(
    base_state,
    own_integral,
    near_list,
    stiffness,
    star_mats,
    face_proj,
    face_lift,
    face_rotate,
    flux_own,
    flux_across,
    across_face,
    rotation,
):
    result = base_state + volume(own_integral, stiffness, star_mats)
    result = result - local_faces(own_integral, face_proj, face_lift, flux_own)
    return result - neighbour_faces(
        near_list, across_face, rotation, face_proj, face_lift, face_rotate, flux_across
    )


def route_blocks(payload, send_list):
    basis_count, field_count = (payload.shape[0], payload.shape[1])
    sub_count = lax.axis_size("sub")
    peer_count = 3 * sub_count
    block_rows = send_list.shape[0] // peer_count
    block_width = basis_count * field_count * block_rows
    outgoing = jnp.take(payload, send_list, axis=2).reshape(
        basis_count, field_count, peer_count, block_rows
    )
    out_blocks = jnp.transpose(outgoing, (2, 0, 1, 3)).reshape(peer_count, block_width)
    slab_view = out_blocks.reshape(3, sub_count, block_width)
    widened = padded(slab_view, (("dom", 0),), 1)
    arrived = widened[0::2]
    incoming = lax.all_to_all(arrived, "sub", split_axis=1, concat_axis=1, tiled=True)
    received = incoming.reshape(peer_count, block_width)
    shaped = received.reshape(peer_count, basis_count, field_count, block_rows)
    return jnp.transpose(shaped, (1, 2, 0, 3)).reshape(
        basis_count, field_count, peer_count * block_rows
    )


def local(
    dof_state,
    stiffness,
    face_proj,
    face_lift,
    face_rotate,
    jacobians,
    material,
    inv_jacobian,
    flux_own,
    flux_across,
    cluster,
    neighbour,
    across_face,
    rotation,
    send_list,
):
    star_mats = star_of(inv_jacobian, jacobians, material)
    series = taylor(dof_state, stiffness, star_mats)
    first_half = integral(series, 0.0, 1.0)
    second_half = integral(series, 1.0, 2.0)
    is_fine = cluster == 0
    zero_column = jnp.zeros(dof_state.shape[:2] + (1,), jnp.float32)
    ext_first = jnp.concatenate(
        [first_half, route_blocks(first_half, send_list), zero_column], axis=2
    )
    near_first = [jnp.take(ext_first, neighbour[i], axis=2) for i in range(4)]
    coarse_own = first_half + second_half
    stepped = update(
        dof_state,
        first_half,
        near_first,
        stiffness,
        star_mats,
        face_proj,
        face_lift,
        face_rotate,
        flux_own,
        flux_across,
        across_face,
        rotation,
    )
    second_step = integral(taylor(stepped, stiffness, star_mats), 0.0, 1.0)
    later_half = jnp.where(is_fine, second_step, second_half)
    base_state = jnp.where(is_fine, stepped, dof_state)
    own_integral = jnp.where(is_fine, second_step, coarse_own)
    ext_later = jnp.concatenate(
        [later_half, route_blocks(later_half, send_list), zero_column], axis=2
    )
    fine_mask = is_fine[None, None, :]
    near_list = []
    for i in range(4):
        near_later = jnp.take(ext_later, neighbour[i], axis=2)
        near_list.append(jnp.where(fine_mask, near_later, near_first[i] + near_later))
    return update(
        base_state,
        own_integral,
        near_list,
        stiffness,
        star_mats,
        face_proj,
        face_lift,
        face_rotate,
        flux_own,
        flux_across,
        across_face,
        rotation,
    )


def solution(mesh):
    in_specs = (
        P(None, None, ("dom", "sub")),
        P(),
        P(),
        P(),
        P(),
        P(),
        P(("dom", "sub")),
        P(None, None, ("dom", "sub")),
        P(None, None, None, ("dom", "sub")),
        P(None, None, None, ("dom", "sub")),
        P(("dom", "sub")),
        P(None, ("dom", "sub")),
        P(None, ("dom", "sub")),
        P(None, ("dom", "sub")),
        P(("dom", "sub")),
    )
    out_specs = P(None, None, ("dom", "sub"))
    return jax.shard_map(local, mesh=mesh, in_specs=in_specs, out_specs=out_specs, check_vma=False)
```

profile of v0, /device:TPU:16, one launch (start us, length us, event | category | flops | bytes accessed | tf_op | source)
XLA Modules:
  0.0 153.5 jit_solution(10122706674649365941)
XLA Ops:
  1.3 1.4 fusion.115
  2.8 1.4 fusion.128
  4.2 1.4 fusion.143
  5.6 0.8 slice_bitcast_fusion.5
  6.4 0.9 copy.377
  19.2 0.9 slice.245
  20.1 2.0 %collective-permute-start = (f32[1,2,4032]{2,1,0:T(2,128)}, f32[1,2,4032]{2,1,0:T(2,128)}, u32[]{:S(2)}, u32[]{:S(2)}) collective-permute-start(f32[1,2,4032]{2,1,0:T(2,128)} %slice.245), channel_id=1, source_target_pairs={{0,2},{2,4},{4,6},{6,8},{8,10},{10,12},{12,14},{14,16},{16,18},{18... | collective-permute-start | bytes 96776 | tf_op jit(solution)/shard_map/ppermute | solution.py:19
  22.6 0.9 slice.247
  23.4 17.0 %collective-permute-start.1 = (f32[1,2,4032]{2,1,0:T(2,128)}, f32[1,2,4032]{2,1,0:T(2,128)}, u32[]{:S(2)}, u32[]{:S(2)}) collective-permute-start(f32[1,2,4032]{2,1,0:T(2,128)} %slice.247), channel_id=1, source_target_pairs={{2,0},{4,2},{6,4},{8,6},{10,8},{12,10},{14,12},{16,14},{18,16},{20... | collective-permute-start | bytes 96776 | tf_op jit(solution)/shard_map/ppermute | solution.py:22
  41.1 0.9 broadcast_select_fusion.1
  46.9 0.8 fusion.202
  50.2 1.2 fusion.13
  51.4 2.2 %copy.396 = f32[6,56,9,8]{3,2,1,0:T(8,128)S(1)} copy(f32[6,56,9,8]{1,2,3,0:T(8,128)} %bitcast.443) | data formatting | bytes 193536 | tf_op jit(solution)/shard_map/transpose | solution.py:146
  53.5 1.4 reshape_reshape.12
  54.9 1.0 pad_maximum_fusion
  56.6 3.4 %all-to-all-start = ((f32[3,2,4032]{2,0,1:T(4,128)}), f32[3,2,4032]{2,0,1:T(4,128)S(1)}, u32[]{:S(2)}, u32[]{:S(2)}) async-start(f32[3,2,4032]{2,0,1:T(4,128)} %copy.398), calls=%async_computation | async-start | bytes 262144 | tf_op jit(solution)/shard_map/all_to_all | solution.py:150
  60.7 0.8 copy.496
  61.5 1.4 copy.494
  62.9 0.8 copy.495
  63.7 1.4 copy.493
  65.8 1.6 %reshape_reshape.13 = f32[6,56,9,8]{3,2,1,0:T(8,128)S(1)} reshape(f32[3,2,4032]{2,1,0:T(2,128)} %copy.399) | data formatting | bytes 193536 | tf_op jit(solution)/shard_map/reshape;reshape | solution.py:152
  67.4 1.6 %copy.400 = f32[56,9,6,8]{0,3,2,1:T(8,128)} copy(f32[56,9,6,8]{3,1,0,2:T(8,128)S(1)} %bitcast.441) | data formatting | bytes 193536 | tf_op jit(solution)/shard_map/transpose | solution.py:153
  69.1 1.1 copy.401
  70.2 1.0 maximum_maximum_fusion
  71.2 1.0 copy.402
  72.1 0.8 gather_fusion.4
  72.9 1.0 copy.412
  73.9 0.8 gather_fusion.3
  74.7 1.0 copy.409
  75.7 1.0 gather_fusion.2
  76.8 1.0 copy.406
  77.8 1.0 gather_fusion.1
  79.2 2.4 %fusion.3 = f32[21,9,128]{2,0,1:T(8,128)S(1)} fusion(f32[12,21,56,1]{2,1,3,0:T(8,128)} %bitcast.466, f32[12,128]{1,0:T(8,128)S(1)} %copy-done.61, f32[128,56,9]{0,1,2:T(8,128)} %copy.412, pred[128]{0:T(512)(128)(4,1)S(1)} %copy-done.78), kind=kOutput, calls=%fused_computation.57 | convolution fusion | flops 195705216 | bytes 417536 | tf_op jit(solution)/shard_map/gx,xqe->gqe/dot_general | solution.py:107
  81.7 2.1 %fusion.2 = f32[21,9,128]{2,0,1:T(8,128)S(1)} fusion(f32[12,21,56,1]{2,1,3,0:T(8,128)} %bitcast.467, f32[12,128]{1,0:T(8,128)S(1)} %copy-done.59, f32[128,56,9]{0,1,2:T(8,128)S(1)} %copy-done.45, pred[128]{0:T(512)(128)(4,1)S(1)} %copy-done.76), kind=kOutput, calls=%fused_computation.56 | convolution fusion | flops 195705216 | bytes 417536 | tf_op jit(solution)/shard_map/gx,xqe->gqe/dot_general | solution.py:107
  84.0 1.2 fusion
  85.3 1.2 fusion.1
  98.6 1.3 multiply_reduce_fusion
  101.3 0.9 broadcast_select_fusion
  105.3 0.9 slice.270
  106.2 1.9 %collective-permute-start.2 = (f32[1,2,4032]{2,1,0:T(2,128)}, f32[1,2,4032]{2,1,0:T(2,128)}, u32[]{:S(2)}, u32[]{:S(2)}) collective-permute-start(f32[1,2,4032]{2,1,0:T(2,128)} %slice.270), channel_id=1, source_target_pairs={{0,2},{2,4},{4,6},{6,8},{8,10},{10,12},{12,14},{14,16},{16,18},{18... | collective-permute-start | bytes 96776 | tf_op jit(solution)/shard_map/ppermute | solution.py:19
  108.6 0.9 slice.272
  109.4 4.5 %collective-permute-start.3 = (f32[1,2,4032]{2,1,0:T(2,128)}, f32[1,2,4032]{2,1,0:T(2,128)}, u32[]{:S(2)}, u32[]{:S(2)}) collective-permute-start(f32[1,2,4032]{2,1,0:T(2,128)} %slice.272), channel_id=1, source_target_pairs={{2,0},{4,2},{6,4},{8,6},{10,8},{12,10},{14,12},{16,14},{18,16},{20... | collective-permute-start | bytes 96776 | tf_op jit(solution)/shard_map/ppermute | solution.py:22
  114.4 1.1 fusion.11
  116.2 2.2 %copy.423 = f32[6,56,9,8]{3,2,1,0:T(8,128)S(1)} copy(f32[6,56,9,8]{1,2,3,0:T(8,128)} %bitcast.444) | data formatting | bytes 193536 | tf_op jit(solution)/shard_map/transpose | solution.py:146
  118.4 0.7 reshape_reshape.14
  119.2 0.9 pad_maximum_fusion.1
  120.7 3.5 %all-to-all-start.1 = ((f32[3,2,4032]{2,0,1:T(4,128)}), f32[3,2,4032]{2,0,1:T(4,128)S(1)}, u32[]{:S(2)}, u32[]{:S(2)}) async-start(f32[3,2,4032]{2,0,1:T(4,128)} %copy.425), calls=%async_computation.1 | async-start | bytes 262144 | tf_op jit(solution)/shard_map/all_to_all | solution.py:150
  124.3 2.2 %fusion.9 = f32[56,9,128]{2,0,1:T(8,128)} fusion(f32[56,9,128]{2,0,1:T(8,128)S(1)} %copy-done.23, f32[21,9,128]{2,0,1:T(8,128)} %multiply_reduce_fusion.40, f32[21,9,128]{2,0,1:T(8,128)} %multiply_reduce_fusion.41, f32[21,9,128]{2,0,1:T(8,128)} %multiply_reduce_fusion.42, f32[21,9,128]{2,0,1:T(8,128)S(1)} %copy-done.39, f32[56,84]{0,1:T(8,128)S(1)} %reshape.251), kind=kOutput, calls=%fused_computation.67 | convolution fusion | flops 65382912 | bytes 921984 | tf_op jit(solution)/shard_map/bg,gpe->bpe/dot_general | solution.py:82
  126.5 2.2 %all-to-all-done.1 = f32[3,2,4032]{2,0,1:T(4,128)S(1)} async-done(((f32[3,2,4032]{2,0,1:T(4,128)}), f32[3,2,4032]{2,0,1:T(4,128)S(1)}, u32[]{:S(2)}, u32[]{:S(2)}) %all-to-all-start.1) | async-done | bytes 96800 | tf_op jit(solution)/shard_map/all_to_all | solution.py:150
  129.5 1.7 %copy.427 = f32[56,9,6,8]{0,3,2,1:T(8,128)} copy(f32[56,9,6,8]{3,1,0,2:T(8,128)S(1)} %bitcast.442) | data formatting | bytes 193536 | tf_op jit(solution)/shard_map/transpose | solution.py:153
  131.2 1.1 copy.428
  132.3 1.0 copy.429
  133.3 2.0 %gather_fusion.9 = f32[128,56,9]{1,2,0:T(8,128)} fusion(f32[56,9,177]{0,1,2:T(8,128)S(1)} %copy.429, s32[1024]{0:T(1024)} %copy-done.64), kind=kCustom, calls=%fused_computation.9.clone | custom fusion | bytes 516608 | tf_op jit(solution)/shard_map/jit(_take)/gather | solution.py:210
  135.3 1.9 %gather_fusion.8 = f32[128,56,9]{1,2,0:T(8,128)} fusion(f32[56,9,177]{0,1,2:T(8,128)S(1)} %copy.429, s32[1024]{0:T(1024)} %copy-done.65), kind=kCustom, calls=%fused_computation.8.clone | custom fusion | bytes 516608 | tf_op jit(solution)/shard_map/jit(_take)/gather | solution.py:210
  137.3 2.0 %gather_fusion.7 = f32[128,56,9]{1,2,0:T(8,128)} fusion(f32[56,9,177]{0,1,2:T(8,128)S(1)} %copy.429, s32[1024]{0:T(1024)} %pad_clamp_fusion.2), kind=kCustom, calls=%fused_computation.7.clone | custom fusion | bytes 516608 | tf_op jit(solution)/shard_map/jit(_take)/gather | solution.py:210
  139.3 1.0 gather_fusion.6
  140.3 1.5 copy.436
  141.8 1.2 fusion.7
  143.2 1.5 copy.434
  144.7 2.2 %fusion.6 = f32[21,9,128]{2,0,1:T(8,128)S(1)} fusion(f32[12,21,56,1]{2,1,3,0:T(8,128)} %bitcast.468, f32[12,128]{1,0:T(8,128)S(1)} %copy-done.60, f32[128,56,9]{0,1,2:T(8,128)S(1)} %copy.434, f32[128,56,9]{0,1,2:T(8,128)S(1)} %copy-done.46, pred[128]{0:T(512)(128)(4,1)S(1)} %copy-done.77, pred[128]{0:T(512)(128)(4,1)S(1)} %copy-done.67), kind=kOutput, calls=%fused_computation.60 | convolution fusion | flops 195898752 | bytes 675712 | tf_op jit(solution)/shard_map/gx,xqe->gqe/dot_general | solution.py:107
  147.1 1.0 copy.432
  148.1 2.3 %fusion.5 = f32[21,9,128]{2,0,1:T(8,128)S(1)} fusion(f32[12,21,56,1]{2,1,3,0:T(8,128)S(1)} %bitcast.472, f32[12,128]{1,0:T(8,128)S(1)} %copy-done.58, f32[128,56,9]{0,1,2:T(8,128)} %copy.432, f32[128,56,9]{0,1,2:T(8,128)} %copy.406, pred[128]{0:T(512)(128)(4,1)S(1)} %copy-done.75, pred[128]{0:T(512)(128)(4,1)S(1)} %copy-done.67), kind=kOutput, calls=%fused_computation.59 | convolution fusion | flops 195898752 | bytes 675712 | tf_op jit(solution)/shard_map/gx,xqe->gqe/dot_general | solution.py:107
  150.8 1.2 fusion.4
  152.2 1.2 fusion.8
  (318 shorter events, 43.8 us)
Async XLA Ops:
  0.0 48.7 %copy-start = (f32[3,21,21]{2,1,0:T(8,128)S(1)}, f32[3,21,21]{2,1,0:T(8,128)}, u32[]{:S(2)}) copy-start(f32[3,21,21]{2,1,0:T(8,128)} %param.23) | copy-start | bytes 15880
  0.0 7.4 %copy-start.71 = (s32[128]{0:T(128)S(1)}, s32[128]{0:T(128)}, u32[]{:S(2)}) copy-start(s32[128]{0:T(128)} %param.25) | copy-start | bytes 1540
  8.4 7.6 %copy-start.6 = (f32[56,9,128]{2,0,1:T(8,128)}, f32[56,9,128]{2,0,1:T(8,128)S(1)}, u32[]{:S(2)}) copy-start(f32[56,9,128]{2,0,1:T(8,128)S(1)} %add_negate_fusion.8) | copy-start | bytes 774148
  10.3 5.7 %copy-start.8 = (f32[56,9,128]{2,0,1:T(8,128)}, f32[56,9,128]{2,0,1:T(8,128)S(1)}, u32[]{:S(2)}) copy-start(f32[56,9,128]{2,0,1:T(8,128)S(1)} %add_negate_fusion.7) | copy-start | bytes 774148
  12.2 3.8 %copy-start.10 = (f32[56,9,128]{2,0,1:T(8,128)}, f32[56,9,128]{2,0,1:T(8,128)S(1)}, u32[]{:S(2)}) copy-start(f32[56,9,128]{2,0,1:T(8,128)S(1)} %add_negate_fusion.6) | copy-start | bytes 774148
  14.0 3.2 %copy-start.2 = (f32[56,9,128]{2,0,1:T(8,128)S(1)}, f32[56,9,128]{2,0,1:T(8,128)}, u32[]{:S(2)}) copy-start(f32[56,9,128]{2,0,1:T(8,128)} %param.19) | copy-start | bytes 774148
  17.4 30.4 %copy-start.4 = (f32[56,9,128]{2,0,1:T(8,128)}, f32[56,9,128]{2,0,1:T(8,128)S(1)}, u32[]{:S(2)}) copy-start(f32[56,9,128]{2,0,1:T(8,128)S(1)} %multiply_add_fusion.2) | copy-start | bytes 774148
  19.1 22.8 %copy-start.80 = (s32[128]{0:T(128)S(1)}, s32[128]{0:T(128)}, u32[]{:S(2)}) copy-start(s32[128]{0:T(128)} %param.29) | copy-start | bytes 1540
  19.1 23.3 %copy-start.68 = (s32[4,128]{1,0:T(4,128)S(1)}, s32[4,128]{1,0:T(4,128)}, u32[]{:S(2)}) copy-start(s32[4,128]{1,0:T(4,128)} %param.30) | copy-start | bytes 6148
  19.1 25.1 %copy-start.69 = (s32[4,128]{1,0:T(4,128)S(1)}, s32[4,128]{1,0:T(4,128)}, u32[]{:S(2)}) copy-start(s32[4,128]{1,0:T(4,128)} %param.31) | copy-start | bytes 6148
  19.2 25.1 %copy-start.70 = (s32[4,128]{1,0:T(4,128)S(1)}, s32[4,128]{1,0:T(4,128)}, u32[]{:S(2)}) copy-start(s32[4,128]{1,0:T(4,128)} %param.32) | copy-start | bytes 6148
  19.2 27.5 %copy-start.54 = (f32[4,56,21]{1,0,2:T(4,128)S(1)}, f32[4,56,21]{1,0,2:T(4,128)}, u32[]{:S(2)}) copy-start(f32[4,56,21]{1,0,2:T(4,128)} %param.22) | copy-start | bytes 56452
  20.1 26.6 %copy-start.48 = (f32[4,21,56]{2,0,1:T(4,128)S(1)}, f32[4,21,56]{2,0,1:T(4,128)}, u32[]{:S(2)}) copy-start(f32[4,21,56]{2,0,1:T(4,128)} %param.21) | copy-start | bytes 56452
  20.1 26.6 %copy-start.49 = (f32[4,9,9,128]{3,0,2,1:T(4,128)S(1)}, f32[4,9,9,128]{3,0,2,1:T(4,128)}, u32[]{:S(2)}) copy-start(f32[4,9,9,128]{3,0,2,1:T(4,128)} %param.27) | copy-start | bytes 497668
  20.1 34.8 %collective-permute-start = (f32[1,2,4032]{2,1,0:T(2,128)}, f32[1,2,4032]{2,1,0:T(2,128)}, u32[]{:S(2)}, u32[]{:S(2)}) collective-permute-start(f32[1,2,4032]{2,1,0:T(2,128)} %slice.245), channel_id=1, source_target_pairs={{0,2},{2,4},{4,6},{6,8},{8,10},{10,12},{12,14},{14,16},{16,18},{18... | collective-permute-start | bytes 96776 | tf_op jit(solution)/shard_map/ppermute | solution.py:19
  22.5 24.4 %copy-start.50 = (f32[4,9,9,128]{3,0,2,1:T(4,128)S(1)}, f32[4,9,9,128]{3,0,2,1:T(4,128)}, u32[]{:S(2)}) copy-start(f32[4,9,9,128]{3,0,2,1:T(4,128)} %param.28) | copy-start | bytes 497668
  23.4 31.5 %collective-permute-start.1 = (f32[1,2,4032]{2,1,0:T(2,128)}, f32[1,2,4032]{2,1,0:T(2,128)}, u32[]{:S(2)}, u32[]{:S(2)}) collective-permute-start(f32[1,2,4032]{2,1,0:T(2,128)} %slice.247), channel_id=1, source_target_pairs={{2,0},{4,2},{6,4},{8,6},{10,8},{12,10},{14,12},{16,14},{18,16},{20... | collective-permute-start | bytes 96776 | tf_op jit(solution)/shard_map/ppermute | solution.py:22
  46.8 2.9 %copy-start.35 = (f32[1,9,9,128]{3,2,1,0:T(8,128)}, f32[1,9,9,128]{3,2,1,0:T(8,128)S(1)}, u32[]{:S(2)}) copy-start(f32[1,9,9,128]{3,2,1,0:T(8,128)S(1)} %copy.500) | copy-start | bytes 124420
  51.4 20.8 %copy-start.64 = (s32[1024]{0:T(1024)}, s32[1024]{0:T(1024)S(1)}, u32[]{:S(2)}) copy-start(s32[1024]{0:T(1024)S(1)} %pad_clamp_fusion) | copy-start | bytes 12292
  56.6 8.5 %all-to-all-start = ((f32[3,2,4032]{2,0,1:T(4,128)}), f32[3,2,4032]{2,0,1:T(4,128)S(1)}, u32[]{:S(2)}, u32[]{:S(2)}) async-start(f32[3,2,4032]{2,0,1:T(4,128)} %copy.398), calls=%async_computation | async-start | bytes 262144 | tf_op jit(solution)/shard_map/all_to_all | solution.py:150
  60.0 13.9 %copy-start.65 = (s32[1024]{0:T(1024)}, s32[1024]{0:T(1024)S(1)}, u32[]{:S(2)}) copy-start(s32[1024]{0:T(1024)S(1)} %pad_clamp_fusion.1) | copy-start | bytes 12292
  75.7 3.5 %copy-start.61 = (f32[12,128]{1,0:T(8,128)S(1)}, f32[12,128]{1,0:T(8,128)}, u32[]{:S(2)}) copy-start(f32[12,128]{1,0:T(8,128)} %fusion.184) | copy-start | bytes 18436
  75.7 3.5 %copy-start.78 = (pred[128]{0:T(512)(128)(4,1)S(1)}, pred[128]{0:T(512)(128)(4,1)}, u32[]{:S(2)}) copy-start(pred[128]{0:T(512)(128)(4,1)} %get-tuple-element.65) | copy-start | bytes 388
  76.7 4.8 %copy-start.31 = (f32[1,9,9,128]{3,2,1,0:T(8,128)S(1)}, f32[1,9,9,128]{3,2,1,0:T(8,128)}, u32[]{:S(2)}) copy-start(f32[1,9,9,128]{3,2,1,0:T(8,128)} %copy.493) | copy-start | bytes 124420
  76.7 4.9 %copy-start.59 = (f32[12,128]{1,0:T(8,128)S(1)}, f32[12,128]{1,0:T(8,128)}, u32[]{:S(2)}) copy-start(f32[12,128]{1,0:T(8,128)} %fusion.183) | copy-start | bytes 18436
  76.8 4.9 %copy-start.76 = (pred[128]{0:T(512)(128)(4,1)S(1)}, pred[128]{0:T(512)(128)(4,1)}, u32[]{:S(2)}) copy-start(pred[128]{0:T(512)(128)(4,1)} %get-tuple-element.67) | copy-start | bytes 388
  77.8 6.1 %copy-start.27 = (f32[1,9,9,128]{3,2,1,0:T(8,128)S(1)}, f32[1,9,9,128]{3,2,1,0:T(8,128)}, u32[]{:S(2)}) copy-start(f32[1,9,9,128]{3,2,1,0:T(8,128)} %copy.494) | copy-start | bytes 124420
  77.8 6.2 %copy-start.55 = (f32[12,128]{1,0:T(8,128)S(1)}, f32[12,128]{1,0:T(8,128)}, u32[]{:S(2)}) copy-start(f32[12,128]{1,0:T(8,128)} %fusion.181) | copy-start | bytes 18436
  77.8 6.2 %copy-start.72 = (pred[128]{0:T(512)(128)(4,1)S(1)}, pred[128]{0:T(512)(128)(4,1)}, u32[]{:S(2)}) copy-start(pred[128]{0:T(512)(128)(4,1)} %get-tuple-element.16) | copy-start | bytes 388
  78.8 2.9 %copy-start.45 = (f32[128,56,9]{0,1,2:T(8,128)S(1)}, f32[128,56,9]{0,1,2:T(8,128)}, u32[]{:S(2)}) copy-start(f32[128,56,9]{0,1,2:T(8,128)} %copy.409) | copy-start | bytes 774148
  78.8 5.2 %copy-start.51 = (f32[3,4,21,56]{3,2,1,0:T(8,128)S(1)}, f32[3,4,21,56]{3,2,1,0:T(8,128)}, u32[]{:S(2)}) copy-start(f32[3,4,21,56]{3,2,1,0:T(8,128)} %copy.392) | copy-start | bytes 169348
  78.8 6.5 %copy-start.44 = (f32[128,56,9]{0,1,2:T(8,128)S(1)}, f32[128,56,9]{0,1,2:T(8,128)}, u32[]{:S(2)}) copy-start(f32[128,56,9]{0,1,2:T(8,128)} %copy.406) | copy-start | bytes 774148
  78.8 6.5 %copy-start.57 = (f32[12,128]{1,0:T(8,128)S(1)}, f32[12,128]{1,0:T(8,128)}, u32[]{:S(2)}) copy-start(f32[12,128]{1,0:T(8,128)} %fusion.182) | copy-start | bytes 18436
  78.8 6.5 %copy-start.74 = (pred[128]{0:T(512)(128)(4,1)S(1)}, pred[128]{0:T(512)(128)(4,1)}, u32[]{:S(2)}) copy-start(pred[128]{0:T(512)(128)(4,1)} %get-tuple-element.63) | copy-start | bytes 388
  79.2 7.3 %copy-start.42 = (f32[128,56,9]{0,1,2:T(8,128)}, f32[128,56,9]{0,1,2:T(8,128)S(1)}, u32[]{:S(2)}) copy-start(f32[128,56,9]{0,1,2:T(8,128)S(1)} %copy.403) | copy-start | bytes 774148
  79.2 7.4 %copy-start.25 = (f32[56,9,128]{2,0,1:T(8,128)S(1)}, f32[56,9,128]{2,0,1:T(8,128)}, u32[]{:S(2)}) copy-start(f32[56,9,128]{2,0,1:T(8,128)} %fusion.13) | copy-start | bytes 774148
  99.9 3.0 %copy-start.38 = (f32[1,9,9,128]{3,2,1,0:T(8,128)S(1)}, f32[1,9,9,128]{3,2,1,0:T(8,128)}, u32[]{:S(2)}) copy-start(f32[1,9,9,128]{3,2,1,0:T(8,128)} %copy-done.37) | copy-start | bytes 124420
  99.9 3.7 %copy-start.34 = (f32[1,9,9,128]{3,2,1,0:T(8,128)S(1)}, f32[1,9,9,128]{3,2,1,0:T(8,128)}, u32[]{:S(2)}) copy-start(f32[1,9,9,128]{3,2,1,0:T(8,128)} %copy-done.33) | copy-start | bytes 124420
  101.2 3.2 %copy-start.24 = (f32[56,9,128]{2,0,1:T(8,128)S(1)}, f32[56,9,128]{2,0,1:T(8,128)}, u32[]{:S(2)}) copy-start(f32[56,9,128]{2,0,1:T(8,128)} %get-tuple-element.9) | copy-start | bytes 774148
  105.3 10.2 %copy-start.30 = (f32[1,9,9,128]{3,2,1,0:T(8,128)S(1)}, f32[1,9,9,128]{3,2,1,0:T(8,128)}, u32[]{:S(2)}) copy-start(f32[1,9,9,128]{3,2,1,0:T(8,128)} %copy-done.29) | copy-start | bytes 124420
  106.2 12.9 %collective-permute-start.2 = (f32[1,2,4032]{2,1,0:T(2,128)}, f32[1,2,4032]{2,1,0:T(2,128)}, u32[]{:S(2)}, u32[]{:S(2)}) collective-permute-start(f32[1,2,4032]{2,1,0:T(2,128)} %slice.270), channel_id=1, source_target_pairs={{0,2},{2,4},{4,6},{6,8},{8,10},{10,12},{12,14},{14,16},{16,18},{18... | collective-permute-start | bytes 96776 | tf_op jit(solution)/shard_map/ppermute | solution.py:19
  109.4 9.7 %collective-permute-start.3 = (f32[1,2,4032]{2,1,0:T(2,128)}, f32[1,2,4032]{2,1,0:T(2,128)}, u32[]{:S(2)}, u32[]{:S(2)}) collective-permute-start(f32[1,2,4032]{2,1,0:T(2,128)} %slice.272), channel_id=1, source_target_pairs={{2,0},{4,2},{6,4},{8,6},{10,8},{12,10},{14,12},{16,14},{18,16},{20... | collective-permute-start | bytes 96776 | tf_op jit(solution)/shard_map/ppermute | solution.py:22
  118.4 5.9 %copy-start.23 = (f32[56,9,128]{2,0,1:T(8,128)S(1)}, f32[56,9,128]{2,0,1:T(8,128)}, u32[]{:S(2)}) copy-start(f32[56,9,128]{2,0,1:T(8,128)} %fusion.11) | copy-start | bytes 774148
  118.4 5.9 %copy-start.39 = (f32[21,9,128]{2,0,1:T(8,128)S(1)}, f32[21,9,128]{2,0,1:T(8,128)}, u32[]{:S(2)}) copy-start(f32[21,9,128]{2,0,1:T(8,128)} %multiply_reduce_fusion.43) | copy-start | bytes 290308
  120.7 8.0 %all-to-all-start.1 = ((f32[3,2,4032]{2,0,1:T(4,128)}), f32[3,2,4032]{2,0,1:T(4,128)S(1)}, u32[]{:S(2)}, u32[]{:S(2)}) async-start(f32[3,2,4032]{2,0,1:T(4,128)} %copy.425), calls=%async_computation.1 | async-start | bytes 262144 | tf_op jit(solution)/shard_map/all_to_all | solution.py:150
  133.3 8.5 %copy-start.47 = (f32[128,56,9]{0,1,2:T(8,128)S(1)}, f32[128,56,9]{0,1,2:T(8,128)}, u32[]{:S(2)}) copy-start(f32[128,56,9]{0,1,2:T(8,128)} %copy.412) | copy-start | bytes 774148
  133.3 8.5 %copy-start.52 = (f32[3,4,21,56]{3,2,1,0:T(8,128)S(1)}, f32[3,4,21,56]{3,2,1,0:T(8,128)}, u32[]{:S(2)}) copy-start(f32[3,4,21,56]{3,2,1,0:T(8,128)} %copy.392) | copy-start | bytes 169348
  133.3 8.5 %copy-start.62 = (f32[12,128]{1,0:T(8,128)S(1)}, f32[12,128]{1,0:T(8,128)}, u32[]{:S(2)}) copy-start(f32[12,128]{1,0:T(8,128)} %fusion.184) | copy-start | bytes 18436
  133.3 8.5 %copy-start.67 = (pred[128]{0:T(512)(128)(4,1)S(1)}, pred[128]{0:T(512)(128)(4,1)}, u32[]{:S(2)}) copy-start(pred[128]{0:T(512)(128)(4,1)} %broadcast_compare_fusion) | copy-start | bytes 388
  133.3 8.5 %copy-start.79 = (pred[128]{0:T(512)(128)(4,1)S(1)}, pred[128]{0:T(512)(128)(4,1)}, u32[]{:S(2)}) copy-start(pred[128]{0:T(512)(128)(4,1)} %get-tuple-element.65) | copy-start | bytes 388
  137.2 5.8 %copy-start.32 = (f32[1,9,9,128]{3,2,1,0:T(8,128)S(1)}, f32[1,9,9,128]{3,2,1,0:T(8,128)}, u32[]{:S(2)}) copy-start(f32[1,9,9,128]{3,2,1,0:T(8,128)} %copy.493) | copy-start | bytes 124420
  139.2 5.4 %copy-start.46 = (f32[128,56,9]{0,1,2:T(8,128)S(1)}, f32[128,56,9]{0,1,2:T(8,128)}, u32[]{:S(2)}) copy-start(f32[128,56,9]{0,1,2:T(8,128)} %copy.409) | copy-start | bytes 774148
  139.2 5.4 %copy-start.60 = (f32[12,128]{1,0:T(8,128)S(1)}, f32[12,128]{1,0:T(8,128)}, u32[]{:S(2)}) copy-start(f32[12,128]{1,0:T(8,128)} %fusion.183) | copy-start | bytes 18436
  139.3 5.5 %copy-start.77 = (pred[128]{0:T(512)(128)(4,1)S(1)}, pred[128]{0:T(512)(128)(4,1)}, u32[]{:S(2)}) copy-start(pred[128]{0:T(512)(128)(4,1)} %get-tuple-element.67) | copy-start | bytes 388
  140.3 6.7 %copy-start.28 = (f32[1,9,9,128]{3,2,1,0:T(8,128)S(1)}, f32[1,9,9,128]{3,2,1,0:T(8,128)}, u32[]{:S(2)}) copy-start(f32[1,9,9,128]{3,2,1,0:T(8,128)} %copy.494) | copy-start | bytes 124420
  141.8 5.2 %copy-start.22 = (f32[128,56,9]{1,2,0:T(8,128)S(1)}, f32[128,56,9]{1,2,0:T(8,128)}, u32[]{:S(2)}) copy-start(f32[128,56,9]{1,2,0:T(8,128)} %gather_fusion.7) | copy-start | bytes 774148
  143.1 5.0 %copy-start.58 = (f32[12,128]{1,0:T(8,128)S(1)}, f32[12,128]{1,0:T(8,128)}, u32[]{:S(2)}) copy-start(f32[12,128]{1,0:T(8,128)} %fusion.182) | copy-start | bytes 18436
  143.1 5.0 %copy-start.75 = (pred[128]{0:T(512)(128)(4,1)S(1)}, pred[128]{0:T(512)(128)(4,1)}, u32[]{:S(2)}) copy-start(pred[128]{0:T(512)(128)(4,1)} %get-tuple-element.63) | copy-start | bytes 388
  143.2 4.9 %copy-start.53 = (f32[3,4,21,56]{3,2,1,0:T(8,128)S(1)}, f32[3,4,21,56]{3,2,1,0:T(8,128)}, u32[]{:S(2)}) copy-start(f32[3,4,21,56]{3,2,1,0:T(8,128)} %copy.392) | copy-start | bytes 169348
  144.7 6.0 %copy-start.43 = (f32[128,56,9]{0,1,2:T(8,128)S(1)}, f32[128,56,9]{0,1,2:T(8,128)}, u32[]{:S(2)}) copy-start(f32[128,56,9]{0,1,2:T(8,128)} %copy-done.42) | copy-start | bytes 774148
  144.7 6.0 %copy-start.56 = (f32[12,128]{1,0:T(8,128)S(1)}, f32[12,128]{1,0:T(8,128)}, u32[]{:S(2)}) copy-start(f32[12,128]{1,0:T(8,128)} %fusion.181) | copy-start | bytes 18436
  144.7 6.0 %copy-start.73 = (pred[128]{0:T(512)(128)(4,1)S(1)}, pred[128]{0:T(512)(128)(4,1)}, u32[]{:S(2)}) copy-start(pred[128]{0:T(512)(128)(4,1)} %get-tuple-element.16) | copy-start | bytes 388
  147.0 6.3 %copy-start.1 = (f32[3,21,21]{2,1,0:T(8,128)S(1)}, f32[3,21,21]{2,1,0:T(8,128)}, u32[]{:S(2)}) copy-start(f32[3,21,21]{2,1,0:T(8,128)} %param.23) | copy-start | bytes 15880
  148.1 4.1 %copy-start.26 = (f32[56,9,128]{2,0,1:T(8,128)S(1)}, f32[56,9,128]{2,0,1:T(8,128)}, u32[]{:S(2)}) copy-start(f32[56,9,128]{2,0,1:T(8,128)} %fusion.9) | copy-start | bytes 774148
  (23 other events, 44.3 us)
where the time goes:
time: 157 us; the launch traced here: 154 us
  local copies, waits for them, and re-layouts  54.1 us (34%)
  matrix products  39.3 us (25%)
  starting transfers between devices  32.4 us (21%)
  other arithmetic  23.3 us (15%)
  waiting for transfers between devices  2.24 us (1%)
  between operations  2.21 us (1%)
    ppermute x2, starting transfers between devices, padded(): lax.ppermute(lax.slice_in_dim(block, 0, width, axis=dim), axis, backward)  21.6 us
    dot_general x30, matrix products, derivative(): moved = jnp.einsum('xb,xqe->bqe', stiffness[dim_d], state, precision=HIGH)  15.8 us
    dot_general x8, matrix products, neighbour_faces(): projected = jnp.einsum('gx,xqe->gqe', combos, near, precision=HIGH)  13.8 us
    reduce_sum x47, other arithmetic, mix_fields(): return jnp.sum(data[:, :, None, :] * mats[None], axis=1)  11.3 us
    gather x8, local copies, waits for them, and re-layouts, local(): near_later = jnp.take(ext_later, neighbour[i], axis=2)  11.2 us
    unnamed x172, local copies, waits for them, and re-layouts  7.44 us
    all_to_all x2, starting transfers between devices, route_blocks(): lax.all_to_all(arrived, 'sub', split_axis=1, concat_axis=1, tiled=True)  6.92 us
    gather x8, local copies, waits for them, and re-layouts, local(): near_first = [jnp.take(ext_first, neighbour[i], axis=2) for i in range(4)]  6.88 us
  transfers between devices with their start and end apart: 6, of which 1 were waited for; matrix products, arithmetic and copies ran while one was open for 19% of the time, Pallas kernels for 0%

commit v1 on v0

v1 whole, which is shorter than its diff:
```python
import functools
import math

import jax
import jax.numpy as jnp
from jax import lax
from jax.experimental import pallas as pl
from jax.experimental.pallas import tpu as pltpu
from jax.sharding import PartitionSpec as P

ORDER = 6
MESH = pl.DeviceIdType.MESH
F32 = jnp.float32
BF16 = jnp.bfloat16


def split(x):
    hi = x.astype(BF16)
    return hi, (x - hi.astype(F32)).astype(BF16)


def tripled(x):
    hi, lo = split(x)
    return jnp.concatenate([hi, lo, hi], axis=0)


def grown(x, rows):
    if x.shape[0] == rows:
        return x
    return jnp.concatenate([x, jnp.zeros((rows - x.shape[0], x.shape[1]), x.dtype)], axis=0)


def weights(x, depth):
    x = grown(x, depth)
    w = jnp.transpose(jnp.concatenate([x, x, x], axis=0))
    hi, lo = split(w)
    lane = lax.broadcasted_iota(jnp.int32, w.shape, 1)
    return jnp.where(lane < 2 * depth, hi.astype(F32), lo.astype(F32)).astype(BF16)


def dot(a, b):
    return jnp.dot(a, b, preferred_element_type=F32)


def kernel(dims, *refs):
    hbm, refs = refs[:15], refs[15:]
    out_ref, held, refs = refs[0], refs[1:16], refs[16:]
    (
        dof_ref,
        stiff_ref,
        proj_ref,
        lift_ref,
        rot_ref,
        table_ref,
        inv_ref,
        own_ref,
        across_ref,
        material_ref,
        cluster_ref,
        neighbour_ref,
        face_ref,
        turn_ref,
        send_ref,
    ) = held
    (
        sendbuf,
        ghost,
        star,
        state,
        moved,
        proj,
        first,
        second,
        stepped,
        chosen,
        chosen_first,
        solved,
        onehot,
        send_sem,
        recv_sem,
        load_sem,
    ) = refs
    loads = [
        pltpu.make_async_copy(hbm[k], held[k], load_sem.at[k]) for k in range(15)
    ]
    for k in (5, 9, 6, 1, 0, 14, 10, 2, 11, 12, 13, 7, 3, 4, 8):
        loads[k].start()

    def ready(*which):
        for k in which:
            loads[k].wait()

    nb, nf, el, fp, nfaces, slabs, subs, blk = dims
    kb = state.shape[1]
    peers = 3 * subs
    slots = peers * blk
    slab = lax.axis_index("dom")
    sub = lax.axis_index("sub")
    barrier = pltpu.get_barrier_semaphore()

    def each_peer(act):
        for t in (-1, 0, 1):
            for r in range(subs):
                there = slab + t
                valid = (there >= 0) & (there < slabs)
                if t == 0:
                    valid = valid & (sub != r)

                @pl.when(valid)
                def _(t=t, r=r, there=there):
                    act(t, r, there)

    ghost[...] = jnp.zeros(ghost.shape, F32)
    each_peer(
        lambda t, r, there: pl.semaphore_signal(
            barrier, inc=1, device_id=(there, r), device_id_type=MESH
        )
    )

    def copy_to(x, t, r, there):
        slot = (1 - t) * subs + sub
        return pltpu.make_async_remote_copy(
            src_ref=sendbuf.at[x, (t + 1) * subs + r],
            dst_ref=ghost.at[x, slot],
            send_sem=send_sem.at[x, (t + 1) * subs + r],
            recv_sem=recv_sem.at[x, slot],
            device_id=(there, r),
            device_id_type=MESH,
        )

    def arrival(x, t, r, there):
        j = (t + 1) * subs + r
        return pltpu.make_async_remote_copy(
            src_ref=sendbuf.at[x, j],
            dst_ref=ghost.at[x, j],
            send_sem=send_sem.at[x, j],
            recv_sem=recv_sem.at[x, j],
            device_id=(there, r),
            device_id_type=MESH,
        )

    ready(5, 9, 6)
    nmat = table_ref.shape[3]
    rows = lax.broadcasted_iota(jnp.int32, (nmat, el), 0)
    picked = (rows == material_ref[...]).astype(F32).astype(BF16)
    per_elem = []
    for c in range(3):
        hi, lo = split(table_ref[:, :, c, :].reshape(nf * nf, nmat))
        per_elem.append(dot(hi, picked) + dot(lo, picked))
    for d in range(3):
        total = inv_ref[0, d : d + 1, :] * per_elem[0]
        for c in range(1, 3):
            total = total + inv_ref[c, d : d + 1, :] * per_elem[c]
        star[d] = jnp.broadcast_to(total[:, None, :], (nf * nf, 8, el))

    ready(1, 0, 14, 10, 2, 11, 12, 13, 7, 3, 4, 8)
    onerow = lax.broadcasted_iota(jnp.int32, (4 * el, el), 0)
    for i in range(nfaces):
        n = neighbour_ref[i : i + 1, :]
        a = face_ref[i : i + 1, :] * el
        local_key = jnp.where(n < el, a + n, -1)
        ghost_key = jnp.where((n >= el) & (n < el + slots), a + n - el, -1)
        cols = slice(i * el, (i + 1) * el)
        onehot[0, :, cols] = (onerow == local_key).astype(F32).astype(BF16)
        onehot[1, :, cols] = (onerow == ghost_key).astype(F32).astype(BF16)
    send_rows = lax.broadcasted_iota(jnp.int32, (el, slots), 0)
    send_hot = jnp.transpose((send_rows == send_ref[...]).astype(F32)).astype(BF16)

    fb = proj_ref.shape[0]
    kf = -(-fb // 16) * 16
    w_pred = jnp.concatenate([weights(-stiff_ref[d], kb) for d in range(3)], axis=0)
    w_vol = jnp.concatenate(
        [weights(jnp.transpose(stiff_ref[d]), kb) for d in range(3)], axis=0
    )
    by_face = [grown(proj_ref[:, i, :], fp) for i in range(nfaces)]
    w_proj = weights(jnp.transpose(jnp.concatenate(by_face, axis=0)), kb)
    by_face = [grown(lift_ref[:, i, :], fp) for i in range(nfaces)]
    w_lift = weights(jnp.concatenate(by_face, axis=0), nfaces * fp)
    w_rot = jnp.concatenate(
        [
            grown(weights(jnp.transpose(rot_ref[h]), kf), fp)
            for h in range(rot_ref.shape[0])
        ],
        axis=0,
    )

    def send(x, data):
        pad = sendbuf.shape[3] - nf * nb
        full = jnp.concatenate([data, jnp.zeros((pad, el), F32)], axis=0)
        hi, lo = split(full)
        nt = (((1,), (1,)), ((), ()))
        out = lax.dot_general(send_hot, hi, nt, preferred_element_type=F32)
        out = out + lax.dot_general(send_hot, lo, nt, preferred_element_type=F32)
        sendbuf[x] = out.reshape(peers, blk, sendbuf.shape[3])
        if x == 0:
            waits = (subs - 1) + jnp.where(slab > 0, subs, 0) + jnp.where(slab < slabs - 1, subs, 0)
            pl.semaphore_wait(barrier, waits)
        each_peer(lambda t, r, there: copy_to(x, t, r, there).start())

    def fields(load):
        return tripled(jnp.concatenate([load(q) for q in range(nf)], axis=1))

    def vol_part(source, p0, width, init):
        acc = list(init)
        for d in range(3):
            for q in range(nf):
                m = source(d, q).reshape(nb // 8, 8, el)
                for k in range(width):
                    acc[k] = acc[k] + m * star[d, q * nf + p0 + k][None]
        return acc

    step_p = 3

    def spread(slot, q0, res, width):
        for k in range(width):
            for d in range(3):
                moved[slot, d * nf + q0 + k] = res[d * nb : (d + 1) * nb, k * el : (k + 1) * el]

    def predict(load, later_out, first_out):
        zero = jnp.zeros((kb - nb, el), F32)
        for q in range(nf):
            x = load(q)
            first_out[q] = jnp.concatenate([x, zero], axis=0)
            if later_out is not None:
                later_out[q] = jnp.concatenate([x, zero], axis=0)
        for q0 in range(0, nf, step_p):
            rhs = tripled(
                jnp.concatenate([first_out[q0 + k] for k in range(step_p)], axis=1)
            )
            spread(0, q0, dot(w_pred, rhs), step_p)

        def order_step(k, carry):
            fact, power = carry
            fact = fact / (k + 2).astype(F32)
            power = power * 2.0
            c2 = (2.0 * power - 1.0) * fact
            now = lax.rem(k, 2)
            nxt = 1 - now
            for p0 in range(0, nf, step_p):
                zeros = [jnp.zeros((nb // 8, 8, el), F32)] * step_p
                acc = vol_part(lambda d, q: moved[now, d * nf + q], p0, step_p, zeros)
                flat = [a.reshape(nb, el) for a in acc]
                for j in range(step_p):
                    first_out[p0 + j, :nb] += fact * flat[j]
                    if later_out is not None:
                        later_out[p0 + j, :nb] += c2 * flat[j]
                rhs = tripled(
                    jnp.concatenate(
                        [jnp.concatenate([a, zero], axis=0) for a in flat], axis=1
                    )
                )
                spread(nxt, p0, dot(w_pred, rhs), step_p)
            return fact, power

        lax.fori_loop(0, ORDER - 1, order_step, (jnp.float32(1.0), jnp.float32(1.0)))

    def gather(load, which):
        lhs = jnp.concatenate(
            [
                jnp.concatenate([load(a, q) for a in range(4)], axis=1)
                for q in range(nf)
            ],
            axis=0,
        )
        hi, lo = split(lhs)
        return dot(hi, onehot[which]) + dot(lo, onehot[which])

    def ghost_fields(x):
        g = ghost[x].reshape(slots, ghost.shape[3])
        g = jnp.concatenate([g, jnp.zeros((el - slots, ghost.shape[3]), F32)], axis=0)
        t = jnp.transpose(g)
        zero = jnp.zeros((kb - nb, el), F32)
        return lambda q: jnp.concatenate([t[q * nb : (q + 1) * nb], zero], axis=0)

    def face_sum(coef, source, i, p):
        acc = jnp.zeros((fp, el), F32)
        for q in range(nf):
            acc = acc + source(i, q) * coef[q, p, i : i + 1, :]
        return acc

    def update(x, source_proj, own_proj, out):
        near = gather(source_proj, 0)
        for i in range(nfaces):
            for p in range(nf):
                solved[i * fp : (i + 1) * fp, p * el : (p + 1) * el] = face_sum(
                    own_ref, own_proj, i, p
                )
        each_peer(lambda t, r, there: arrival(x, t, r, there).wait_recv())
        res = dot(w_proj, fields(ghost_fields(x)))
        near = near + gather(
            lambda a, q: res[a * fp : (a + 1) * fp, q * el : (q + 1) * el], 1
        )
        zero = jnp.zeros((kf - fp, el), F32)
        for i in range(nfaces):
            turn = turn_ref[i : i + 1, :]
            rhs = tripled(
                jnp.concatenate(
                    [
                        jnp.concatenate(
                            [near[q * fp : (q + 1) * fp, i * el : (i + 1) * el], zero], axis=0
                        )
                        for q in range(nf)
                    ],
                    axis=1,
                )
            )
            turned = dot(w_rot, rhs)
            for q in range(nf):
                cols = slice(q * el, (q + 1) * el)
                got = jnp.where(
                    turn == 0,
                    turned[:fp, cols],
                    jnp.where(turn == 1, turned[fp : 2 * fp, cols], turned[2 * fp :, cols]),
                )
                if x == 0:
                    chosen_first[i * nf + q] = got
                else:
                    got = got + jnp.where(is_fine, 0.0, chosen_first[i * nf + q])
                chosen[i * nf + q] = got
            for p in range(nf):
                cols = slice(p * el, (p + 1) * el)
                solved[i * fp : (i + 1) * fp, cols] += face_sum(
                    across_ref, lambda i, q: chosen[i * nf + q], i, p
                )
        lifted = dot(w_lift, tripled(solved[...]))
        for p in range(nf):
            out[p, :nb] = out[p, :nb] - lifted[:, p * el : (p + 1) * el]

    is_fine = cluster_ref[...] == 0

    predict(lambda q: dof_ref[q], second, first)
    send(0, jnp.concatenate([first[q, :nb] for q in range(nf)], axis=0))

    def volume_into(base, out):
        for p0 in range(0, nf, step_p):
            init = [base(p0 + k).reshape(nb // 8, 8, el) for k in range(step_p)]
            acc = vol_part(lambda d, q: moved[0, d * nf + q], p0, step_p, init)
            for k in range(step_p):
                out[p0 + k, :nb] = acc[k].reshape(nb, el)

    rhs = fields(lambda q: first[q])
    spread(0, 0, dot(w_vol, rhs), nf)
    res = dot(w_proj, rhs)
    for i in range(nfaces):
        for q in range(nf):
            r0 = i * fp
            proj[0, i * nf + q] = res[r0 : r0 + fp, q * el : (q + 1) * el]
    volume_into(lambda p: dof_ref[p], stepped)
    pick = lambda s: lambda i, q: proj[s, i * nf + q]
    update(0, pick(0), pick(0), stepped)

    predict(lambda q: stepped[q, :nb], None, state)
    for q in range(nf):
        second[q] = jnp.where(is_fine, state[q], second[q])
    send(1, jnp.concatenate([second[q, :nb] for q in range(nf)], axis=0))

    res = dot(w_proj, fields(lambda q: second[q]))
    for i in range(nfaces):
        for q in range(nf):
            later = res[i * fp : (i + 1) * fp, q * el : (q + 1) * el]
            proj[1, i * nf + q] = later
            proj[2, i * nf + q] = later + jnp.where(is_fine, 0.0, proj[0, i * nf + q])
    for q in range(nf):
        state[q] = second[q] + jnp.where(is_fine, 0.0, first[q])
    spread(0, 0, dot(w_vol, fields(lambda q: state[q])), nf)
    volume_into(lambda p: jnp.where(is_fine, stepped[p, :nb], dof_ref[p]), out_ref)
    update(1, pick(1), pick(2), out_ref)

    for x in range(2):
        each_peer(lambda t, r, there: copy_to(x, t, r, there).wait_send())


def local(
    slabs,
    subs,
    dof_state,
    stiffness,
    face_proj,
    face_lift,
    face_rotate,
    jacobians,
    material,
    inv_jacobian,
    flux_own,
    flux_across,
    cluster,
    neighbour,
    across_face,
    rotation,
    send_list,
):
    nb, nf, el = dof_state.shape
    nfaces, fb, _ = face_proj.shape
    nmat = jacobians.shape[0]
    blk = send_list.shape[0] // (3 * subs)
    fp = -(-fb // 8) * 8
    kb = -(-nb // 16) * 16
    lanes = -(-nf * nb // 128) * 128
    vmem = pl.BlockSpec(memory_space=pltpu.VMEM)
    args = (
        jnp.transpose(dof_state, (1, 0, 2)),
        stiffness,
        jnp.transpose(face_proj, (1, 0, 2)),
        jnp.transpose(face_lift, (2, 0, 1)),
        face_rotate,
        jnp.transpose(jacobians, (2, 3, 1, 0)),
        inv_jacobian,
        jnp.transpose(flux_own, (1, 2, 0, 3)),
        jnp.transpose(flux_across, (1, 2, 0, 3)),
        material.reshape(1, el),
        cluster.reshape(1, el),
        neighbour,
        across_face,
        rotation,
        send_list.reshape(1, send_list.shape[0]),
    )
    out = pl.pallas_call(
        functools.partial(kernel, (nb, nf, el, fp, nfaces, slabs, subs, blk)),
        out_shape=jax.ShapeDtypeStruct((nf, nb, el), F32),
        in_specs=[pl.BlockSpec(memory_space=pltpu.HBM)] * 15,
        out_specs=vmem,
        scratch_shapes=[pltpu.VMEM(x.shape, x.dtype) for x in args]
        + [
            pltpu.VMEM((2, 3 * subs, blk, lanes), F32),
            pltpu.VMEM((2, 3 * subs, blk, lanes), F32),
            pltpu.VMEM((3, nf * nf, 8, el), F32),
            pltpu.VMEM((nf, kb, el), F32),
            pltpu.VMEM((2, 3 * nf, nb, el), F32),
            pltpu.VMEM((3, nfaces * nf, fp, el), F32),
            pltpu.VMEM((nf, kb, el), F32),
            pltpu.VMEM((nf, kb, el), F32),
            pltpu.VMEM((nf, nb, el), F32),
            pltpu.VMEM((nfaces * nf, fp, el), F32),
            pltpu.VMEM((nfaces * nf, fp, el), F32),
            pltpu.VMEM((nfaces * fp, nf * el), F32),
            pltpu.VMEM((2, 4 * el, nfaces * el), BF16),
            pltpu.SemaphoreType.DMA((2, 3 * subs)),
            pltpu.SemaphoreType.DMA((2, 3 * subs)),
            pltpu.SemaphoreType.DMA((len(args),)),
        ],
        compiler_params=pltpu.CompilerParams(
            collective_id=0, has_side_effects=True, vmem_limit_bytes=64 * 2**20
        ),
    )(
        *args,
    )
    return jnp.transpose(out, (1, 0, 2))


def solution(mesh):
    split_all = ("dom", "sub")
    in_specs = (
        P(None, None, split_all),
        P(),
        P(),
        P(),
        P(),
        P(),
        P(split_all),
        P(None, None, split_all),
        P(None, None, None, split_all),
        P(None, None, None, split_all),
        P(split_all),
        P(None, split_all),
        P(None, split_all),
        P(None, split_all),
        P(split_all),
    )
    return jax.shard_map(
        functools.partial(local, mesh.shape["dom"], mesh.shape["sub"]),
        mesh=mesh,
        in_specs=in_specs,
        out_specs=P(None, None, split_all),
        check_vma=False,
    )
```

time: 157 us -> 27.2 us (0.17)
  the two profiles are of different devices: /device:TPU:16 before, /device:TPU:1 now
where the time goes in v1:
time: 27.2 us; the launch traced here: 27 us
  Pallas kernels  25.3 us (93%)
  local copies, waits for them, and re-layouts  1.66 us (6%)
    pallas_call x1, Pallas kernels, local(): pl.pallas_call(functools.partial(kernel, (nb, nf, el, fp, nfaces, slabs,...  25.3 us
    unnamed x1, local copies, waits for them, and re-layouts  1.66 us

profile of v1, /device:TPU:1, one launch (start us, length us, event | category | flops | bytes accessed | tf_op | source)
XLA Modules:
  0.0 27.0 jit_solution(11117419336455311566)
XLA Ops:
  0.0 25.3 %shard_map.145 = f32[9,56,128]{2,1,0:T(8,128)} custom-call(f32[9,56,128]{2,1,0:T(8,128)} %bitcast.11, f32[3,56,56]{2,1,0:T(8,128)} %refs_1_.1, f32[21,4,56]{2,1,0:T(4,128)} %bitcast.15, f32[21,4,56]{2,1,0:T(4,128)} %bitcast.16, f32[3,21,21]{2,1,0:T(8,128)} %refs_4_.1, f32[9,9,3,16]{3,2,1,0:T(4,128)} %bitcast.12, f32[3,3,128]{2,1,0:T(4,128)} %refs_6_.1, ...), custom_call_target="tpu_custom_call" | custom-call | tf_op jit(solution)/shard_map/pallas_call | solution.py:417
  25.4 1.7 %copy.17 = f32[56,9,128]{2,0,1:T(8,128)} copy(f32[56,9,128]{2,0,1:T(8,128)} %bitcast.10) | data formatting | bytes 516096

commit v2 on v1

--- a/solution.py
+++ b/solution.py
@@ -68,6 +68,7 @@
         star,
         state,
         moved,
+        moved_b,
         proj,
         first,
         second,
@@ -153,37 +154,11 @@
             total = total + inv_ref[c, d : d + 1, :] * per_elem[c]
         star[d] = jnp.broadcast_to(total[:, None, :], (nf * nf, 8, el))
 
-    ready(1, 0, 14, 10, 2, 11, 12, 13, 7, 3, 4, 8)
-    onerow = lax.broadcasted_iota(jnp.int32, (4 * el, el), 0)
-    for i in range(nfaces):
-        n = neighbour_ref[i : i + 1, :]
-        a = face_ref[i : i + 1, :] * el
-        local_key = jnp.where(n < el, a + n, -1)
-        ghost_key = jnp.where((n >= el) & (n < el + slots), a + n - el, -1)
-        cols = slice(i * el, (i + 1) * el)
-        onehot[0, :, cols] = (onerow == local_key).astype(F32).astype(BF16)
-        onehot[1, :, cols] = (onerow == ghost_key).astype(F32).astype(BF16)
+    ready(14, 1, 0, 10)
     send_rows = lax.broadcasted_iota(jnp.int32, (el, slots), 0)
     send_hot = jnp.transpose((send_rows == send_ref[...]).astype(F32)).astype(BF16)
 
-    fb = proj_ref.shape[0]
-    kf = -(-fb // 16) * 16
     w_pred = jnp.concatenate([weights(-stiff_ref[d], kb) for d in range(3)], axis=0)
-    w_vol = jnp.concatenate(
-        [weights(jnp.transpose(stiff_ref[d]), kb) for d in range(3)], axis=0
-    )
-    by_face = [grown(proj_ref[:, i, :], fp) for i in range(nfaces)]
-    w_proj = weights(jnp.transpose(jnp.concatenate(by_face, axis=0)), kb)
-    by_face = [grown(lift_ref[:, i, :], fp) for i in range(nfaces)]
-    w_lift = weights(jnp.concatenate(by_face, axis=0), nfaces * fp)
-    w_rot = jnp.concatenate(
-        [
-            grown(weights(jnp.transpose(rot_ref[h]), kf), fp)
-            for h in range(rot_ref.shape[0])
-        ],
-        axis=0,
-    )
-
     def send(x, data):
         pad = sendbuf.shape[3] - nf * nb
         full = jnp.concatenate([data, jnp.zeros((pad, el), F32)], axis=0)
@@ -202,57 +177,61 @@
 
     def vol_part(source, p0, width, init):
         acc = list(init)
-        for d in range(3):
-            for q in range(nf):
-                m = source(d, q).reshape(nb // 8, 8, el)
+        for q in range(nf):
+            for d in range(3):
+                m = source[d * nf + q].reshape(nb // 8, 8, el)
                 for k in range(width):
                     acc[k] = acc[k] + m * star[d, q * nf + p0 + k][None]
         return acc
 
-    step_p = 3
-
-    def spread(slot, q0, res, width):
+    chunks = [(p0, min(4, nf - p0)) for p0 in range(0, nf, 4)]
+
+    def spread(target, q0, res, width):
         for k in range(width):
             for d in range(3):
-                moved[slot, d * nf + q0 + k] = res[d * nb : (d + 1) * nb, k * el : (k + 1) * el]
+                target[d * nf + q0 + k] = res[d * nb : (d + 1) * nb, k * el : (k + 1) * el]
 
     def predict(load, later_out, first_out):
         zero = jnp.zeros((kb - nb, el), F32)
         for q in range(nf):
-            x = load(q)
-            first_out[q] = jnp.concatenate([x, zero], axis=0)
+            x = grown(load(q), kb)
+            first_out[q] = x
             if later_out is not None:
-                later_out[q] = jnp.concatenate([x, zero], axis=0)
-        for q0 in range(0, nf, step_p):
+                later_out[q] = x
+        for q0, width in chunks:
             rhs = tripled(
-                jnp.concatenate([first_out[q0 + k] for k in range(step_p)], axis=1)
+                jnp.concatenate([grown(load(q0 + k), kb) for k in range(width)], axis=1)
             )
-            spread(0, q0, dot(w_pred, rhs), step_p)
-
-        def order_step(k, carry):
+            spread(moved, q0, dot(w_pred, rhs), width)
+
+        def order_step(k, carry, now, nxt):
             fact, power = carry
             fact = fact / (k + 2).astype(F32)
             power = power * 2.0
             c2 = (2.0 * power - 1.0) * fact
-            now = lax.rem(k, 2)
-            nxt = 1 - now
-            for p0 in range(0, nf, step_p):
-                zeros = [jnp.zeros((nb // 8, 8, el), F32)] * step_p
-                acc = vol_part(lambda d, q: moved[now, d * nf + q], p0, step_p, zeros)
+            for p0, width in chunks:
+                zeros = [jnp.zeros((nb // 8, 8, el), F32)] * width
+                acc = vol_part(now, p0, width, zeros)
                 flat = [a.reshape(nb, el) for a in acc]
-                for j in range(step_p):
+                for j in range(width):
                     first_out[p0 + j, :nb] += fact * flat[j]
                     if later_out is not None:
                         later_out[p0 + j, :nb] += c2 * flat[j]
-                rhs = tripled(
-                    jnp.concatenate(
-                        [jnp.concatenate([a, zero], axis=0) for a in flat], axis=1
+                if nxt is not None:
+                    rhs = tripled(
+                        jnp.concatenate([grown(a, kb) for a in flat], axis=1)
                     )
-                )
-                spread(nxt, p0, dot(w_pred, rhs), step_p)
+                    spread(nxt, p0, dot(w_pred, rhs), width)
             return fact, power
 
-        lax.fori_loop(0, ORDER - 1, order_step, (jnp.float32(1.0), jnp.float32(1.0)))
+        def pair(h, carry):
+            carry = order_step(2 * h, carry, moved, moved_b)
+            return order_step(2 * h + 1, carry, moved_b, moved)
+
+        steps = ORDER - 1
+        carry = (jnp.float32(1.0), jnp.float32(1.0))
+        carry = lax.fori_loop(0, steps // 2, pair, carry)
+        order_step(jnp.int32(steps - 1), carry, moved, None)
 
     def gather(load, which):
         lhs = jnp.concatenate(
@@ -272,25 +251,30 @@
         zero = jnp.zeros((kb - nb, el), F32)
         return lambda q: jnp.concatenate([t[q * nb : (q + 1) * nb], zero], axis=0)
 
-    def face_sum(coef, source, i, p):
-        acc = jnp.zeros((fp, el), F32)
+    def face_sums(coef, source, i):
+        acc = [jnp.zeros((fp, el), F32)] * nf
         for q in range(nf):
-            acc = acc + source(i, q) * coef[q, p, i : i + 1, :]
+            data = source(i, q)
+            for p in range(nf):
+                acc[p] = acc[p] + data * coef[q, p, i : i + 1, :]
         return acc
 
     def update(x, source_proj, own_proj, out):
         near = gather(source_proj, 0)
+        if x == 0:
+            ready(7)
         for i in range(nfaces):
+            sums = face_sums(own_ref, own_proj, i)
             for p in range(nf):
-                solved[i * fp : (i + 1) * fp, p * el : (p + 1) * el] = face_sum(
-                    own_ref, own_proj, i, p
-                )
+                solved[i * fp : (i + 1) * fp, p * el : (p + 1) * el] = sums[p]
+        if x == 0:
+            ready(8)
         each_peer(lambda t, r, there: arrival(x, t, r, there).wait_recv())
         res = dot(w_proj, fields(ghost_fields(x)))
         near = near + gather(
             lambda a, q: res[a * fp : (a + 1) * fp, q * el : (q + 1) * el], 1
         )
-        zero = jnp.zeros((kf - fp, el), F32)
+        zero = jnp.zeros((-(-proj_ref.shape[0] // 16) * 16 - fp, el), F32)
         for i in range(nfaces):
             turn = turn_ref[i : i + 1, :]
             rhs = tripled(
@@ -317,11 +301,9 @@
                 else:
                     got = got + jnp.where(is_fine, 0.0, chosen_first[i * nf + q])
                 chosen[i * nf + q] = got
+            sums = face_sums(across_ref, lambda i, q: chosen[i * nf + q], i)
             for p in range(nf):
-                cols = slice(p * el, (p + 1) * el)
-                solved[i * fp : (i + 1) * fp, cols] += face_sum(
-                    across_ref, lambda i, q: chosen[i * nf + q], i, p
-                )
+                solved[i * fp : (i + 1) * fp, p * el : (p + 1) * el] += sums[p]
         lifted = dot(w_lift, tripled(solved[...]))
         for p in range(nf):
             out[p, :nb] = out[p, :nb] - lifted[:, p * el : (p + 1) * el]
@@ -331,15 +313,42 @@
     predict(lambda q: dof_ref[q], second, first)
     send(0, jnp.concatenate([first[q, :nb] for q in range(nf)], axis=0))
 
+    ready(2, 11, 12, 13, 3, 4)
+    onerow = lax.broadcasted_iota(jnp.int32, (4 * el, el), 0)
+    for i in range(nfaces):
+        n = neighbour_ref[i : i + 1, :]
+        a = face_ref[i : i + 1, :] * el
+        local_key = jnp.where(n < el, a + n, -1)
+        ghost_key = jnp.where((n >= el) & (n < el + slots), a + n - el, -1)
+        cols = slice(i * el, (i + 1) * el)
+        onehot[0, :, cols] = (onerow == local_key).astype(F32).astype(BF16)
+        onehot[1, :, cols] = (onerow == ghost_key).astype(F32).astype(BF16)
+    fb = proj_ref.shape[0]
+    kf = -(-fb // 16) * 16
+    w_vol = jnp.concatenate(
+        [weights(jnp.transpose(stiff_ref[d]), kb) for d in range(3)], axis=0
+    )
+    by_face = [grown(proj_ref[:, i, :], fp) for i in range(nfaces)]
+    w_proj = weights(jnp.transpose(jnp.concatenate(by_face, axis=0)), kb)
+    by_face = [grown(lift_ref[:, i, :], fp) for i in range(nfaces)]
+    w_lift = weights(jnp.concatenate(by_face, axis=0), nfaces * fp)
+    w_rot = jnp.concatenate(
+        [
+            grown(weights(jnp.transpose(rot_ref[h]), kf), fp)
+            for h in range(rot_ref.shape[0])
+        ],
+        axis=0,
+    )
+
     def volume_into(base, out):
-        for p0 in range(0, nf, step_p):
-            init = [base(p0 + k).reshape(nb // 8, 8, el) for k in range(step_p)]
-            acc = vol_part(lambda d, q: moved[0, d * nf + q], p0, step_p, init)
-            for k in range(step_p):
+        for p0, width in chunks:
+            init = [base(p0 + k).reshape(nb // 8, 8, el) for k in range(width)]
+            acc = vol_part(moved, p0, width, init)
+            for k in range(width):
                 out[p0 + k, :nb] = acc[k].reshape(nb, el)
 
     rhs = fields(lambda q: first[q])
-    spread(0, 0, dot(w_vol, rhs), nf)
+    spread(moved, 0, dot(w_vol, rhs), nf)
     res = dot(w_proj, rhs)
     for i in range(nfaces):
         for q in range(nf):
@@ -362,7 +371,7 @@
             proj[2, i * nf + q] = later + jnp.where(is_fine, 0.0, proj[0, i * nf + q])
     for q in range(nf):
         state[q] = second[q] + jnp.where(is_fine, 0.0, first[q])
-    spread(0, 0, dot(w_vol, fields(lambda q: state[q])), nf)
+    spread(moved, 0, dot(w_vol, fields(lambda q: state[q])), nf)
     volume_into(lambda p: jnp.where(is_fine, stepped[p, :nb], dof_ref[p]), out_ref)
     update(1, pick(1), pick(2), out_ref)
 
@@ -416,7 +425,7 @@
     )
     out = pl.pallas_call(
         functools.partial(kernel, (nb, nf, el, fp, nfaces, slabs, subs, blk)),
-        out_shape=jax.ShapeDtypeStruct((nf, nb, el), F32),
+        out_shape=pltpu.VMEM((nf, nb, el), F32),
         in_specs=[pl.BlockSpec(memory_space=pltpu.HBM)] * 15,
         out_specs=vmem,
         scratch_shapes=[pltpu.VMEM(x.shape, x.dtype) for x in args]
@@ -425,7 +434,8 @@
             pltpu.VMEM((2, 3 * subs, blk, lanes), F32),
             pltpu.VMEM((3, nf * nf, 8, el), F32),
             pltpu.VMEM((nf, kb, el), F32),
-            pltpu.VMEM((2, 3 * nf, nb, el), F32),
+            pltpu.VMEM((3 * nf, nb, el), F32),
+            pltpu.VMEM((3 * nf, nb, el), F32),
             pltpu.VMEM((3, nfaces * nf, fp, el), F32),
             pltpu.VMEM((nf, kb, el), F32),
             pltpu.VMEM((nf, kb, el), F32),
@@ -439,10 +449,10 @@
             pltpu.SemaphoreType.DMA((len(args),)),
         ],
         compiler_params=pltpu.CompilerParams(
-            collective_id=0, has_side_effects=True, vmem_limit_bytes=64 * 2**20
+            collective_id=0, has_side_effects=True, vmem_limit_bytes=48 * 2**20
         ),
     )(
-        *args,
+        *[pltpu.with_memory_space_constraint(x, pltpu.HBM) for x in args],
     )
     return jnp.transpose(out, (1, 0, 2))
 

time: 27.2 us -> 20.6 us (0.76)
  Pallas kernels: 25.3 us -> 19.8 us
  local copies, waits for them, and re-layouts: 1.66 us -> 0.7 us
    pallas_call x1, Pallas kernels: 25.3 us -> 19.8 us  [local(): pl.pallas_call(functools.partial(kernel, (nb, nf, el, fp, nfaces, slabs,...]
    unnamed x1, local copies, waits for them, and re-layouts: 1.66 us -> 0.7 us
where the time goes in v2:
time: 20.6 us; the launch traced here: 20.5 us
  Pallas kernels  19.8 us (96%)
  local copies, waits for them, and re-layouts  0.7 us (3%)
    pallas_call x1, Pallas kernels, local(): pl.pallas_call(functools.partial(kernel, (nb, nf, el, fp, nfaces, slabs,...  19.8 us
    unnamed x1, local copies, waits for them, and re-layouts  0.7 us

profile of v2, /device:TPU:1, one launch (start us, length us, event | category | flops | bytes accessed | tf_op | source)
XLA Modules:
  0.0 20.5 jit_solution(7645619111343574171)
XLA Ops:
  0.0 19.8 %shard_map.145 = f32[9,56,128]{2,1,0:T(8,128)S(1)} custom-call(f32[9,56,128]{2,1,0:T(8,128)} %bitcast.11, f32[3,56,56]{2,1,0:T(8,128)} %refs_1_.1, f32[21,4,56]{2,1,0:T(4,128)} %bitcast.15, f32[21,4,56]{2,1,0:T(4,128)} %bitcast.16, f32[3,21,21]{2,1,0:T(8,128)} %refs_4_.1, f32[9,9,3,16]{3,2,1,0:T(4,128)} %bitcast.12, f32[3,3,128]{2,1,0:T(4,128)} %refs_6_.1, ...), custom_call_target="tpu_custom_call" | custom-call | tf_op jit(solution)/shard_map/pallas_call | solution.py:426
  19.8 0.7 %copy.17 = f32[56,9,128]{2,0,1:T(8,128)} copy(f32[56,9,128]{2,0,1:T(8,128)S(1)} %bitcast.10) | data formatting | bytes 516096

commit v3 on v2

--- a/solution.py
+++ b/solution.py
@@ -77,6 +77,7 @@
         chosen_first,
         solved,
         onehot,
+        ghost_hot,
         send_sem,
         recv_sem,
         load_sem,
@@ -233,20 +234,22 @@
         carry = lax.fori_loop(0, steps // 2, pair, carry)
         order_step(jnp.int32(steps - 1), carry, moved, None)
 
-    def gather(load, which):
+    def gather(load, hot):
         lhs = jnp.concatenate(
             [
-                jnp.concatenate([load(a, q) for a in range(4)], axis=1)
+                jnp.concatenate([load(a, q) for a in range(hot.shape[0] // el)], axis=1)
                 for q in range(nf)
             ],
             axis=0,
         )
-        hi, lo = split(lhs)
-        return dot(hi, onehot[which]) + dot(lo, onehot[which])
+        rows = -(-nf * fp // 16) * 16
+        hi, lo = split(grown(lhs, rows))
+        both = dot(jnp.concatenate([hi, lo], axis=0), hot[...])
+        return both[: nf * fp] + both[rows : rows + nf * fp]
 
     def ghost_fields(x):
         g = ghost[x].reshape(slots, ghost.shape[3])
-        g = jnp.concatenate([g, jnp.zeros((el - slots, ghost.shape[3]), F32)], axis=0)
+        g = jnp.concatenate([grown(g, el)], axis=0)
         t = jnp.transpose(g)
         zero = jnp.zeros((kb - nb, el), F32)
         return lambda q: jnp.concatenate([t[q * nb : (q + 1) * nb], zero], axis=0)
@@ -260,7 +263,7 @@
         return acc
 
     def update(x, source_proj, own_proj, out):
-        near = gather(source_proj, 0)
+        near = gather(source_proj, onehot)
         if x == 0:
             ready(7)
         for i in range(nfaces):
@@ -269,42 +272,46 @@
                 solved[i * fp : (i + 1) * fp, p * el : (p + 1) * el] = sums[p]
         if x == 0:
             ready(8)
+        def turn_by(parts, turn):
+            rhs = tripled(jnp.concatenate([grown(part, kf) for part in parts], axis=1))
+            turned = dot(w_rot, rhs)
+            result = []
+            for q in range(nf):
+                cols = slice(q * el, (q + 1) * el)
+                last = jnp.where(turn == 1, turned[fp : 2 * fp, cols], turned[2 * fp :, cols])
+                result.append(jnp.where(turn == 0, turned[:fp, cols], last))
+            return result
+
+        for i in range(nfaces):
+            cols = slice(i * el, (i + 1) * el)
+            parts = [near[q * fp : (q + 1) * fp, cols] for q in range(nf)]
+            for q, got in enumerate(turn_by(parts, turn_ref[i : i + 1, :])):
+                if x == 1:
+                    got = got + jnp.where(is_fine, 0.0, chosen_first[i * nf + q])
+                chosen[i * nf + q] = got
         each_peer(lambda t, r, there: arrival(x, t, r, there).wait_recv())
         res = dot(w_proj, fields(ghost_fields(x)))
-        near = near + gather(
-            lambda a, q: res[a * fp : (a + 1) * fp, q * el : (q + 1) * el], 1
-        )
-        zero = jnp.zeros((-(-proj_ref.shape[0] // 16) * 16 - fp, el), F32)
+        parts = []
+        for q in range(nf):
+            part = res[:fp, q * el : (q + 1) * el]
+            for a in range(1, nfaces):
+                other = res[a * fp : (a + 1) * fp, q * el : (q + 1) * el]
+                part = jnp.where(slot_face == a, other, part)
+            parts.append(part)
+        turned = turn_by(parts, slot_turn)
+        came = gather(lambda a, q: turned[q], ghost_hot)
         for i in range(nfaces):
-            turn = turn_ref[i : i + 1, :]
-            rhs = tripled(
-                jnp.concatenate(
-                    [
-                        jnp.concatenate(
-                            [near[q * fp : (q + 1) * fp, i * el : (i + 1) * el], zero], axis=0
-                        )
-                        for q in range(nf)
-                    ],
-                    axis=1,
-                )
-            )
-            turned = dot(w_rot, rhs)
             for q in range(nf):
-                cols = slice(q * el, (q + 1) * el)
-                got = jnp.where(
-                    turn == 0,
-                    turned[:fp, cols],
-                    jnp.where(turn == 1, turned[fp : 2 * fp, cols], turned[2 * fp :, cols]),
-                )
+                got = chosen[i * nf + q]
+                got = got + came[q * fp : (q + 1) * fp, i * el : (i + 1) * el]
+                chosen[i * nf + q] = got
                 if x == 0:
                     chosen_first[i * nf + q] = got
-                else:
-                    got = got + jnp.where(is_fine, 0.0, chosen_first[i * nf + q])
-                chosen[i * nf + q] = got
             sums = face_sums(across_ref, lambda i, q: chosen[i * nf + q], i)
             for p in range(nf):
                 solved[i * fp : (i + 1) * fp, p * el : (p + 1) * el] += sums[p]
-        lifted = dot(w_lift, tripled(solved[...]))
+        lifted = dot(w_lift, jnp.concatenate(split(solved[...]), axis=0))
+        lifted = lifted[:nb] + lifted[nb:]
         for p in range(nf):
             out[p, :nb] = out[p, :nb] - lifted[:, p * el : (p + 1) * el]
 
@@ -314,24 +321,44 @@
     send(0, jnp.concatenate([first[q, :nb] for q in range(nf)], axis=0))
 
     ready(2, 11, 12, 13, 3, 4)
+    ghost_row = lax.broadcasted_iota(jnp.int32, ghost_hot.shape[:1] + (el,), 0)
     onerow = lax.broadcasted_iota(jnp.int32, (4 * el, el), 0)
     for i in range(nfaces):
         n = neighbour_ref[i : i + 1, :]
         a = face_ref[i : i + 1, :] * el
         local_key = jnp.where(n < el, a + n, -1)
-        ghost_key = jnp.where((n >= el) & (n < el + slots), a + n - el, -1)
+        ghost_key = jnp.where((n >= el) & (n < el + slots), n - el, -1)
         cols = slice(i * el, (i + 1) * el)
-        onehot[0, :, cols] = (onerow == local_key).astype(F32).astype(BF16)
-        onehot[1, :, cols] = (onerow == ghost_key).astype(F32).astype(BF16)
+        onehot[:, cols] = (onerow == local_key).astype(F32).astype(BF16)
+        ghost_hot[:, cols] = (ghost_row == ghost_key).astype(F32).astype(BF16)
     fb = proj_ref.shape[0]
     kf = -(-fb // 16) * 16
+    keys = jnp.concatenate(
+        [
+            jnp.concatenate([ref[i : i + 1, :] for i in range(nfaces)], axis=1)
+            for ref in (face_ref, turn_ref)
+        ],
+        axis=0,
+    )
+    slot_keys = lax.dot_general(
+        grown(keys.astype(F32), 16).astype(BF16),
+        ghost_hot[...],
+        (((1,), (1,)), ((), ())),
+        preferred_element_type=F32,
+    )
+    slot_face, slot_turn = slot_keys[0:1], slot_keys[1:2]
+
     w_vol = jnp.concatenate(
         [weights(jnp.transpose(stiff_ref[d]), kb) for d in range(3)], axis=0
     )
     by_face = [grown(proj_ref[:, i, :], fp) for i in range(nfaces)]
     w_proj = weights(jnp.transpose(jnp.concatenate(by_face, axis=0)), kb)
     by_face = [grown(lift_ref[:, i, :], fp) for i in range(nfaces)]
-    w_lift = weights(jnp.concatenate(by_face, axis=0), nfaces * fp)
+    lift = jnp.concatenate(by_face, axis=0)
+    hi, lo = split(jnp.transpose(jnp.concatenate([lift, lift], axis=0)))
+    lane = lax.broadcasted_iota(jnp.int32, lo.shape, 1)
+    lo = jnp.where(lane < nfaces * fp, lo.astype(F32), 0.0)
+    w_lift = jnp.concatenate([hi.astype(F32), lo], axis=0).astype(BF16)
     w_rot = jnp.concatenate(
         [
             grown(weights(jnp.transpose(rot_ref[h]), kf), fp)
@@ -443,7 +470,8 @@
             pltpu.VMEM((nfaces * nf, fp, el), F32),
             pltpu.VMEM((nfaces * nf, fp, el), F32),
             pltpu.VMEM((nfaces * fp, nf * el), F32),
-            pltpu.VMEM((2, 4 * el, nfaces * el), BF16),
+            pltpu.VMEM((4 * el, nfaces * el), BF16),
+            pltpu.VMEM((el, nfaces * el), BF16),
             pltpu.SemaphoreType.DMA((2, 3 * subs)),
             pltpu.SemaphoreType.DMA((2, 3 * subs)),
             pltpu.SemaphoreType.DMA((len(args),)),

time: 20.6 us -> 20.4 us (level)
  Pallas kernels: 19.8 us -> 19.5 us
    pallas_call x1, Pallas kernels: 19.8 us -> 19.5 us  [local(): pl.pallas_call(functools.partial(kernel, (nb, nf, el, fp, nfaces, slabs,...]
where the time goes in v3:
time: 20.4 us; the launch traced here: 20.2 us
  Pallas kernels  19.5 us (96%)
  local copies, waits for them, and re-layouts  0.7 us (3%)
    pallas_call x1, Pallas kernels, local(): pl.pallas_call(functools.partial(kernel, (nb, nf, el, fp, nfaces, slabs,...  19.5 us
    unnamed x1, local copies, waits for them, and re-layouts  0.7 us

profile of v3, /device:TPU:1, one launch (start us, length us, event | category | flops | bytes accessed | tf_op | source)
XLA Modules:
  0.0 20.2 jit_solution(9761888895720631662)
XLA Ops:
  0.0 19.5 %shard_map.145 = f32[9,56,128]{2,1,0:T(8,128)S(1)} custom-call(f32[9,56,128]{2,1,0:T(8,128)} %bitcast.11, f32[3,56,56]{2,1,0:T(8,128)} %refs_1_.1, f32[21,4,56]{2,1,0:T(4,128)} %bitcast.15, f32[21,4,56]{2,1,0:T(4,128)} %bitcast.16, f32[3,21,21]{2,1,0:T(8,128)} %refs_4_.1, f32[9,9,3,16]{3,2,1,0:T(4,128)} %bitcast.12, f32[3,3,128]{2,1,0:T(4,128)} %refs_6_.1, ...), custom_call_target="tpu_custom_call" | custom-call | tf_op jit(solution)/shard_map/pallas_call | solution.py:453
  19.5 0.7 %copy.17 = f32[56,9,128]{2,0,1:T(8,128)} copy(f32[56,9,128]{2,0,1:T(8,128)S(1)} %bitcast.10) | data formatting | bytes 516096
